TPU v7x, 32 devices: a whole 2x2x4 slice. The times are simulated.
32 devices in a mesh: batch: 1, blk: 4 (over x, core), box: 8 (over z, y).
Axes of the slice: x: 2, y: 2, z: 4, core: 2. Of those that a mesh axis runs over, the one named last changes fastest.
Arguments:
- surface_points: float32 [3, 4096], P(None, ('blk', 'box')), may hold values from -4 to 4
- angle_ids: int32 [128], P('batch'), may hold values from 0 to 16383
- near_mask: int32 [32, 8], P(('blk', 'box')), may hold values 0 or 1
- skeleton: int32 [32, 32], P(('blk', 'box')), may hold values from 0 to 127, as said below
- box_inverse_parts: float32 [32, 2, 128, 128], P(('blk', 'box')), may hold values from -0.375 to 0.375
- near_coupling: float32 [32, 8, 2, 32, 128], P(('blk', 'box')), may hold values from -0.25 to 0.25
- top_inverse: float32 [4, 2, 256, 256], P('blk', None, 'box'), may hold values from -0.25 to 0.25
Outputs:
- scattered: float32 [2, 128, 4096], P(None, ('batch', 'box'), 'blk')
Inputs may be any that keep to these rules, and one draw needn't show every extreme that they name: `skeleton`: each row holds 32 distinct row numbers of a box.
All inputs are finite; a program needn't handle non-finite values. No bound on the sum of `near_mask` on one device may be relied on, other than what follows from the above.
Results may differ from a plain program's by a relative error of at most 0.0003.
Values sent between devices are 32-bit elements; how exact they have to be, the bound alone decides.
A program may use at most 64 MiB of HBM per device.

v0:
```python
import functools

import jax
import jax.numpy as jnp
from jax import lax
from jax.experimental import pallas as pl
from jax.experimental.pallas import tpu as pltpu
from jax.sharding import PartitionSpec as P

SWEEP = 16384
WAVENUMBER = 24.0
OFFSETS = ((-1, -1), (-1, 0), (-1, 1), (0, -1), (0, 1), (1, -1), (1, 0), (1, 1))
MESH = pl.DeviceIdType.MESH
F32 = jnp.float32
BF16 = jnp.bfloat16


def sin_cos(x):
    n = jnp.round(x * (2.0 / jnp.pi))
    r = x - n * 1.5703125
    r = r - n * 4.8375129699707031e-4
    r = r - n * 7.5497899548918822e-8
    s = r * r
    sine = ((-1.9515295891e-4 * s + 8.3321608736e-3) * s - 1.6666654611e-1) * s * r + r
    cosine = ((2.443315711809948e-5 * s - 1.388731625493765e-3) * s + 4.166664568298827e-2) * (
        s * s
    ) + (1.0 - 0.5 * s)
    place = n - 4.0 * jnp.floor(n * 0.25)
    odd = (place == 1.0) | (place == 3.0)
    sin_sign = jnp.where(place >= 2.0, -1.0, 1.0)
    cos_sign = jnp.where((place == 1.0) | (place == 2.0), -1.0, 1.0)
    return sin_sign * jnp.where(odd, cosine, sine), cos_sign * jnp.where(odd, sine, cosine)


def split(x):
    high = x.astype(BF16)
    return high, (x - high.astype(F32)).astype(BF16)


def dot(a, b):
    return jnp.dot(a, b, preferred_element_type=F32)


def dot3(a, b):
    return dot(a[0], b[0]) + (dot(a[0], b[1]) + dot(a[1], b[0]))


def beside(a, b, axis):
    return tuple(jnp.concatenate([a[i], b[i]], axis=axis) for i in range(2))


def kernel(
    n_blk,
    n_box,
    points_hbm,
    angles_hbm,
    mask_hbm,
    skeleton_hbm,
    l_hbm,
    e_hbm,
    g_hbm,
    out_ref,
    points_ref,
    angles_ref,
    mask_ref,
    skeleton_ref,
    l_ref,
    e_ref,
    g_ref,
    u_ref,
    near_ref,
    t_ref,
    x_ref,
    load_sem,
    u_send,
    u_recv,
    t_send,
    t_recv,
    x_send,
    x_recv,
):
    r = lax.axis_index("blk")
    q = lax.axis_index("box")
    width = l_ref.shape[1]
    rank = u_ref.shape[1]
    count = u_ref.shape[2]
    share = count // n_box

    def around(dr, dq):
        return {"blk": lax.rem(r + dr + n_blk, n_blk), "box": lax.rem(q + dq + n_box, n_box)}

    loads = [
        pltpu.make_async_copy(angles_hbm, angles_ref, load_sem.at[0]),
        pltpu.make_async_copy(points_hbm, points_ref, load_sem.at[1]),
        pltpu.make_async_copy(l_hbm.at[0], l_ref, load_sem.at[2]),
        pltpu.make_async_copy(e_hbm.at[0], e_ref, load_sem.at[3]),
        pltpu.make_async_copy(skeleton_hbm, skeleton_ref, load_sem.at[5]),
        pltpu.make_async_copy(mask_hbm, mask_ref, load_sem.at[6]),
        pltpu.make_async_copy(g_hbm.at[0], g_ref, load_sem.at[4]),
    ]
    for load in loads:
        load.start()

    barrier = pltpu.get_barrier_semaphore()
    greeted = [around(0, d) for d in range(1, n_box)]
    greeted += [around(dr, dq) for dr, dq in OFFSETS if dr != 0]
    for device in greeted:
        pl.semaphore_signal(barrier, inc=1, device_id=device, device_id_type=MESH)

    loads[0].wait()
    loads[1].wait()
    theta = angles_ref[...].astype(F32) * (2.0 * jnp.pi / SWEEP)
    sin_theta, cos_theta = sin_cos(theta)

    def column(i):
        return jnp.broadcast_to(points_ref[i : i + 1, :], (count, width)).T

    phase = WAVENUMBER * (
        column(0) * cos_theta + column(1) * (0.6 * sin_theta) + column(2) * (0.8 * sin_theta)
    )
    sine, cosine = sin_cos(phase)

    half = count // 2
    first = lax.broadcasted_iota(jnp.int32, (1, count), 1) < half

    def turned(a):
        return jnp.where(first, -1.0, 1.0) * pltpu.roll(a, half, 1)

    def both(a):
        return split(jnp.concatenate([a, turned(a)], axis=0))

    def both_transposed(a):
        return split(jnp.concatenate([a.T, turned(a).T], axis=1))

    field = [
        both(jnp.where(first, cosine, pltpu.roll(sine, half, 1))),
        both(jnp.where(first, pltpu.roll(cosine, half, 1), sine)),
    ]

    loads[4].wait()
    row = lax.broadcasted_iota(jnp.int32, (rank, width), 0)
    lane = lax.broadcasted_iota(jnp.int32, (rank, width), 1)
    wanted = jnp.zeros((rank, width), jnp.int32)
    for k in range(rank):
        wanted = jnp.where(row == k, skeleton_ref[0, k], wanted)
    picker = jnp.where(wanted == lane, 1.0, 0.0).astype(BF16)

    def pick(a):
        return tuple(dot(picker, half).astype(BF16) for half in a)

    loads[2].wait()
    lr, li = split(l_ref[0]), split(l_ref[1])
    plr, pli = pick(lr), pick(li)
    picked = beside(plr, pli, 1)
    u = [dot3(picked, part) for part in field]
    for h in range(2):
        u_ref[h] = u[h]

    pl.semaphore_wait(barrier, len(greeted))

    u_copies = [[], []]
    for h in range(2):
        for m, (dr, dq) in enumerate(OFFSETS):
            copy = pltpu.make_async_remote_copy(
                src_ref=u_ref.at[h],
                dst_ref=near_ref.at[h, 7 - m],
                send_sem=u_send.at[h, m],
                recv_sem=u_recv.at[h, 7 - m],
                device_id=around(dr, dq),
                device_id_type=MESH,
            )
            copy.start()
            u_copies[h].append(copy)

    whole = beside(lr, li, 1)
    z = [dot3(whole, part) for part in field]
    loads[3].wait()
    loads[5].wait()
    masked = [
        e_ref[m] * mask_ref[0, m].astype(F32) for m in range(len(OFFSETS))
    ]
    er = split(jnp.concatenate([e[0] for e in masked], axis=0).T)
    ei = split(jnp.concatenate([e[1] for e in masked], axis=0).T)
    coupling = beside(er, ei, 1)
    picked_coupling = beside(pick(er), pick(ei), 1)
    loads[6].wait()
    top = beside(split(g_ref[0]), split(g_ref[1]), 1)

    t_copies = [[], []]
    near = []
    for h in range(2):
        for copy in u_copies[h]:
            copy.wait_recv()
        near.append(both(near_ref[h].reshape(len(OFFSETS) * rank, count)))
        t_ref[h, pl.ds(q, 1)] = (u[h] - dot3(picked_coupling, near[h])).reshape(1, rank, count)
        for d in range(1, n_box):
            copy = pltpu.make_async_remote_copy(
                src_ref=t_ref.at[h, q],
                dst_ref=t_ref.at[h, q],
                send_sem=t_send.at[h, d],
                recv_sem=t_recv.at[h, d],
                device_id=around(0, d),
                device_id_type=MESH,
            )
            copy.start()
            t_copies[h].append(copy)

    below = beside(lr, li, 0)
    picked_below = beside(plr, pli, 0)
    x = [
        dot3(both_transposed(z[h] - dot3(coupling, near[h])), below) for h in range(2)
    ]

    here = pl.ds(pl.multiple_of(q * width, width), width)
    places = n_box // 2

    def send_x(to):
        d = lax.rem(to - q + n_box, n_box)
        return pltpu.make_async_remote_copy(
            src_ref=x_ref.at[to // places, :, pl.ds(to % places * share, share)],
            dst_ref=out_ref.at[:, :, here],
            send_sem=x_send.at[to],
            recv_sem=x_recv.at[d],
            device_id={"blk": r, "box": to},
            device_id_type=MESH,
        )

    for h in range(2):
        for copy in t_copies[h]:
            copy.wait_recv()
        y = dot3(top, both(t_ref[h].reshape(n_box * rank, count)))
        x_ref[h] = (x[h] + dot3(both_transposed(y), picked_below)).reshape(2, half, width)
        for to in range(h * places, h * places + places):

            @pl.when(q != to)
            def _(to=to):
                send_x(to).start()

    start = pl.multiple_of(lax.rem(q, places) * share, share)
    out_ref[:, :, here] = x_ref[q // places, :, pl.ds(start, share)]

    for d in range(1, n_box):
        pltpu.make_async_remote_copy(
            src_ref=x_ref.at[0, :, pl.ds(0, share)],
            dst_ref=out_ref.at[:, :, pl.ds(pl.multiple_of(lax.rem(q - d + n_box, n_box) * width, width), width)],
            send_sem=x_send.at[0],
            recv_sem=x_recv.at[d],
            device_id=around(0, d),
            device_id_type=MESH,
        ).wait_recv()
    for copy in u_copies[0] + u_copies[1] + t_copies[0] + t_copies[1]:
        copy.wait_send()
    for to in range(n_box):

        @pl.when(q != to)
        def _(to=to):
            send_x(to).wait_send()


def on_device(
    n_blk,
    n_box,
    surface_points,
    angle_ids,
    near_mask,
    skeleton,
    box_inverse_parts,
    near_coupling,
    top_inverse,
):
    width = box_inverse_parts.shape[2]
    count = angle_ids.shape[0]
    rank = skeleton.shape[1]
    vmem = pl.BlockSpec(memory_space=pltpu.VMEM)
    hbm = pl.BlockSpec(memory_space=pl.ANY)
    return pl.pallas_call(
        functools.partial(kernel, n_blk, n_box),
        out_shape=jax.ShapeDtypeStruct((2, count // n_box, n_box * width), F32),
        in_specs=[hbm] * 7,
        out_specs=vmem,
        scratch_shapes=[
            pltpu.VMEM(surface_points.shape, F32),
            pltpu.VMEM((1, count), jnp.int32),
            pltpu.SMEM(near_mask.shape, jnp.int32),
            pltpu.SMEM(skeleton.shape, jnp.int32),
            pltpu.VMEM(box_inverse_parts.shape[1:], F32),
            pltpu.VMEM(near_coupling.shape[1:], F32),
            pltpu.VMEM(top_inverse.shape[1:], F32),
            pltpu.VMEM((2, rank, count), F32),
            pltpu.VMEM((2, len(OFFSETS), rank, count), F32),
            pltpu.VMEM((2, n_box, rank, count), F32),
            pltpu.VMEM((2, 2, count // 2, width), F32),
            pltpu.SemaphoreType.DMA((7,)),
            pltpu.SemaphoreType.DMA((2, len(OFFSETS))),
            pltpu.SemaphoreType.DMA((2, len(OFFSETS))),
            pltpu.SemaphoreType.DMA((2, n_box)),
            pltpu.SemaphoreType.DMA((2, n_box)),
            pltpu.SemaphoreType.DMA((n_box,)),
            pltpu.SemaphoreType.DMA((n_box,)),
        ],
        compiler_params=pltpu.CompilerParams(
            collective_id=0, has_side_effects=True, vmem_limit_bytes=60 * 1024 * 1024
        ),
    )(
        surface_points,
        angle_ids.reshape(1, count),
        near_mask,
        skeleton,
        box_inverse_parts,
        near_coupling,
        top_inverse,
    )


def solution(mesh):
    return jax.shard_map(
        functools.partial(on_device, mesh.shape["blk"], mesh.shape["box"]),
        mesh=mesh,
        in_specs=(
            P(None, ("blk", "box")),
            P("batch"),
            P(("blk", "box"), None),
            P(("blk", "box"), None),
            P(("blk", "box"), None, None, None),
            P(("blk", "box"), None, None, None, None),
            P("blk", None, "box", None),
        ),
        out_specs=P(None, ("batch", "box"), "blk"),
        check_vma=False,
    )
```

profile of v0, /device:TPU:0, one launch (start us, length us, event | category | flops | bytes accessed | tf_op | source)
XLA Modules:
  0.0 26.4 jit_solution(1670294697156072240)
XLA Ops:
  0.0 24.9 %shard_map.73 = f32[2,16,1024]{2,1,0:T(8,128)} custom-call(f32[3,128]{1,0:T(4,128)} %points_hbm.1, s32[1,128]{1,0:T(1,128)} %bitcast.1, s32[1,8]{1,0:T(1,128)} %mask_hbm.1, s32[1,32]{1,0:T(1,128)} %skeleton_hbm.1, f32[1,2,128,128]{3,2,1,0:T(8,128)} %l_hbm.1, f32[1,8,2,32,128]{4,3,2,1,0:T(8,128)} %e_hbm.1, f32[1,2,32,256]{3,2,1,0:T(8,128)} %g_hbm.1), custom_call_target="tpu_custom_call" | custom-call | tf_op jit(solution)/shard_map/pallas_call | solution.py:276
  24.9 1.6 %copy.9 = f32[2,16,1024]{2,1,0:T(8,128)} copy(f32[2,16,1024]{2,1,0:T(8,128)} %shard_map.73) | data formatting | bytes 262144
where the time goes:
time: 26.6 us; the launch traced here: 26.4 us
  Pallas kernels  24.9 us (94%)
  local copies, waits for them, and re-layouts  1.57 us (6%)
    pallas_call x1, Pallas kernels, on_device(): pl.pallas_call(functools.partial(kernel, n_blk, n_box), out_shape=jax.Sha...  24.9 us
    unnamed x1, local copies, waits for them, and re-layouts  1.57 us

commit v1 on v0

--- a/solution.py
+++ b/solution.py
@@ -299,16 +299,21 @@
             pltpu.SemaphoreType.DMA((n_box,)),
         ],
         compiler_params=pltpu.CompilerParams(
-            collective_id=0, has_side_effects=True, vmem_limit_bytes=60 * 1024 * 1024
+            collective_id=0, has_side_effects=True, vmem_limit_bytes=16 * 1024 * 1024
         ),
     )(
-        surface_points,
-        angle_ids.reshape(1, count),
-        near_mask,
-        skeleton,
-        box_inverse_parts,
-        near_coupling,
-        top_inverse,
+        *(
+            pltpu.with_memory_space_constraint(a, pltpu.HBM)
+            for a in (
+                surface_points,
+                angle_ids.reshape(1, count),
+                near_mask,
+                skeleton,
+                box_inverse_parts,
+                near_coupling,
+                top_inverse,
+            )
+        )
     )
 
 

time: 26.6 us -> 25 us (0.940)
  local copies, waits for them, and re-layouts: 1.57 us -> 0.66 us
  Pallas kernels: 24.9 us -> 24.2 us
    unnamed x1, local copies, waits for them, and re-layouts: 1.57 us -> 0.66 us
    pallas_call x1, Pallas kernels: 24.9 us -> 24.2 us  [on_device(): pl.pallas_call(functools.partial(kernel, n_blk, n_box), out_shape=jax.Sha...]
where the time goes in v1:
time: 25 us; the launch traced here: 24.9 us
  Pallas kernels  24.2 us (97%)
  local copies, waits for them, and re-layouts  0.66 us (3%)
    pallas_call x1, Pallas kernels, on_device(): pl.pallas_call(functools.partial(kernel, n_blk, n_box), out_shape=jax.Sha...  24.2 us
    unnamed x1, local copies, waits for them, and re-layouts  0.66 us

profile of v1, /device:TPU:0, one launch (start us, length us, event | category | flops | bytes accessed | tf_op | source)
XLA Modules:
  0.0 24.9 jit_solution(12691298310351352181)
XLA Ops:
  0.0 24.2 %shard_map.73 = f32[2,16,1024]{2,1,0:T(8,128)S(1)} custom-call(f32[3,128]{1,0:T(4,128)} %points_hbm.1, s32[1,128]{1,0:T(1,128)} %bitcast.1, s32[1,8]{1,0:T(1,128)} %mask_hbm.1, s32[1,32]{1,0:T(1,128)} %skeleton_hbm.1, f32[1,2,128,128]{3,2,1,0:T(8,128)} %l_hbm.1, f32[1,8,2,32,128]{4,3,2,1,0:T(8,128)} %e_hbm.1, f32[1,2,32,256]{3,2,1,0:T(8,128)} %g_hbm.1), custom_call_target="tpu_custom_call" | custom-call | tf_op jit(solution)/shard_map/pallas_call | solution.py:276
  24.2 0.7 %copy.9 = f32[2,16,1024]{2,1,0:T(8,128)} copy(f32[2,16,1024]{2,1,0:T(8,128)S(1)} %shard_map.73) | data formatting | bytes 262144

commit v2 on v1

--- a/solution.py
+++ b/solution.py
@@ -89,6 +89,15 @@
     def around(dr, dq):
         return {"blk": lax.rem(r + dr + n_blk, n_blk), "box": lax.rem(q + dq + n_box, n_box)}
 
+    def across(k):
+        place = q
+        bit = 1
+        while bit <= k:
+            if k & bit:
+                place = place + bit - 2 * bit * lax.rem(q // bit, 2)
+            bit *= 2
+        return {"blk": r, "box": place}
+
     loads = [
         pltpu.make_async_copy(angles_hbm, angles_ref, load_sem.at[0]),
         pltpu.make_async_copy(points_hbm, points_ref, load_sem.at[1]),
@@ -199,7 +208,7 @@
                 dst_ref=t_ref.at[h, q],
                 send_sem=t_send.at[h, d],
                 recv_sem=t_recv.at[h, d],
-                device_id=around(0, d),
+                device_id=across(d),
                 device_id_type=MESH,
             )
             copy.start()

time: 25 us -> 24.1 us (0.964)
  Pallas kernels: 24.2 us -> 23.2 us
    pallas_call x1, Pallas kernels: 24.2 us -> 23.2 us  [on_device(): pl.pallas_call(functools.partial(kernel, n_blk, n_box), out_shape=jax.Sha...]
where the time goes in v2:
time: 24.1 us; the launch traced here: 23.9 us
  Pallas kernels  23.2 us (96%)
  local copies, waits for them, and re-layouts  0.66 us (3%)
    pallas_call x1, Pallas kernels, on_device(): pl.pallas_call(functools.partial(kernel, n_blk, n_box), out_shape=jax.Sha...  23.2 us
    unnamed x1, local copies, waits for them, and re-layouts  0.66 us

profile of v2, /device:TPU:0, one launch (start us, length us, event | category | flops | bytes accessed | tf_op | source)
XLA Modules:
  0.0 23.9 jit_solution(15604773259671444856)
XLA Ops:
  0.0 23.2 %shard_map.73 = f32[2,16,1024]{2,1,0:T(8,128)S(1)} custom-call(f32[3,128]{1,0:T(4,128)} %points_hbm.1, s32[1,128]{1,0:T(1,128)} %bitcast.1, s32[1,8]{1,0:T(1,128)} %mask_hbm.1, s32[1,32]{1,0:T(1,128)} %skeleton_hbm.1, f32[1,2,128,128]{3,2,1,0:T(8,128)} %l_hbm.1, f32[1,8,2,32,128]{4,3,2,1,0:T(8,128)} %e_hbm.1, f32[1,2,32,256]{3,2,1,0:T(8,128)} %g_hbm.1), custom_call_target="tpu_custom_call" | custom-call | tf_op jit(solution)/shard_map/pallas_call | solution.py:285
  23.3 0.7 %copy.9 = f32[2,16,1024]{2,1,0:T(8,128)} copy(f32[2,16,1024]{2,1,0:T(8,128)S(1)} %shard_map.73) | data formatting | bytes 262144

commit v3 on v2

--- a/solution.py
+++ b/solution.py
@@ -69,13 +69,22 @@
     g_ref,
     u_ref,
     near_ref,
+    mine_ref,
     t_ref,
+    p_ref,
+    above_ref,
+    other_ref,
     x_ref,
+    came_ref,
     load_sem,
     u_send,
     u_recv,
     t_send,
     t_recv,
+    pair_send,
+    pair_recv,
+    w_send,
+    w_recv,
     x_send,
     x_recv,
 ):
@@ -85,6 +94,10 @@
     rank = u_ref.shape[1]
     count = u_ref.shape[2]
     share = count // n_box
+    half = count // 2
+    pairs = n_box // 2
+    pair = q // 2
+    side = lax.rem(q, 2)
 
     def around(dr, dq):
         return {"blk": lax.rem(r + dr + n_blk, n_blk), "box": lax.rem(q + dq + n_box, n_box)}
@@ -105,7 +118,7 @@
         pltpu.make_async_copy(e_hbm.at[0], e_ref, load_sem.at[3]),
         pltpu.make_async_copy(skeleton_hbm, skeleton_ref, load_sem.at[5]),
         pltpu.make_async_copy(mask_hbm, mask_ref, load_sem.at[6]),
-        pltpu.make_async_copy(g_hbm.at[0], g_ref, load_sem.at[4]),
+        pltpu.make_async_copy(g_hbm.at[0], g_ref.at[0], load_sem.at[4]),
     ]
     for load in loads:
         load.start()
@@ -118,7 +131,15 @@
 
     loads[0].wait()
     loads[1].wait()
-    theta = angles_ref[...].astype(F32) * (2.0 * jnp.pi / SWEEP)
+    given = angles_ref[...].astype(F32)
+    block = lax.broadcasted_iota(jnp.int32, (1, count), 1) // share
+    theta = given
+    for j in range(n_box):
+        source = 2 * j if j < pairs else 2 * (j - pairs) + 1
+        if source != j:
+            moved = pltpu.roll(given, (j - source) % n_box * share, 1)
+            theta = jnp.where(block == j, moved, theta)
+    theta = theta * (2.0 * jnp.pi / SWEEP)
     sin_theta, cos_theta = sin_cos(theta)
 
     def column(i):
@@ -129,7 +150,6 @@
     )
     sine, cosine = sin_cos(phase)
 
-    half = count // 2
     first = lax.broadcasted_iota(jnp.int32, (1, count), 1) < half
 
     def turned(a):
@@ -164,6 +184,8 @@
     u = [dot3(picked, part) for part in field]
     for h in range(2):
         u_ref[h] = u[h]
+    for i, part in enumerate((plr, pli)):
+        p_ref[0, i] = part[0].astype(F32) + part[1].astype(F32)
 
     pl.semaphore_wait(barrier, len(greeted))
 
@@ -181,6 +203,21 @@
             copy.start()
             u_copies[h].append(copy)
 
+    pair_copies = [
+        pltpu.make_async_remote_copy(
+            src_ref=ref.at[0],
+            dst_ref=ref.at[1],
+            send_sem=pair_send.at[i],
+            recv_sem=pair_recv.at[i],
+            device_id=across(1),
+            device_id_type=MESH,
+        )
+        for i, ref in enumerate((g_ref, p_ref))
+    ]
+    loads[6].wait()
+    for copy in pair_copies:
+        copy.start()
+
     whole = beside(lr, li, 1)
     z = [dot3(whole, part) for part in field]
     loads[3].wait()
@@ -192,78 +229,131 @@
     ei = split(jnp.concatenate([e[1] for e in masked], axis=0).T)
     coupling = beside(er, ei, 1)
     picked_coupling = beside(pick(er), pick(ei), 1)
-    loads[6].wait()
-    top = beside(split(g_ref[0]), split(g_ref[1]), 1)
-
-    t_copies = [[], []]
+
+    def send_t(h, d):
+        return pltpu.make_async_remote_copy(
+            src_ref=mine_ref.at[h],
+            dst_ref=t_ref.at[q],
+            send_sem=t_send.at[d],
+            recv_sem=t_recv.at[d],
+            device_id=across(d),
+            device_id_type=MESH,
+        )
+
     near = []
     for h in range(2):
         for copy in u_copies[h]:
             copy.wait_recv()
         near.append(both(near_ref[h].reshape(len(OFFSETS) * rank, count)))
-        t_ref[h, pl.ds(q, 1)] = (u[h] - dot3(picked_coupling, near[h])).reshape(1, rank, count)
+        mine_ref[h] = u[h] - dot3(picked_coupling, near[h])
         for d in range(1, n_box):
-            copy = pltpu.make_async_remote_copy(
-                src_ref=t_ref.at[h, q],
-                dst_ref=t_ref.at[h, q],
-                send_sem=t_send.at[h, d],
-                recv_sem=t_recv.at[h, d],
-                device_id=across(d),
-                device_id_type=MESH,
-            )
-            copy.start()
-            t_copies[h].append(copy)
+
+            @pl.when(lax.rem(q + d, 2) == h)
+            def _(h=h, d=d):
+                send_t(h, d).start()
+
+    t_ref[pl.ds(q, 1)] = mine_ref[pl.ds(side, 1)]
 
     below = beside(lr, li, 0)
-    picked_below = beside(plr, pli, 0)
-    x = [
-        dot3(both_transposed(z[h] - dot3(coupling, near[h])), below) for h in range(2)
-    ]
-
-    here = pl.ds(pl.multiple_of(q * width, width), width)
-    places = n_box // 2
-
-    def send_x(to):
-        d = lax.rem(to - q + n_box, n_box)
+    for h in range(2):
+        above_ref[h] = dot3(
+            both_transposed(z[h] - dot3(coupling, near[h])), below
+        ).reshape(2, half, width)
+
+    def send_w(to):
         return pltpu.make_async_remote_copy(
-            src_ref=x_ref.at[to // places, :, pl.ds(to % places * share, share)],
-            dst_ref=out_ref.at[:, :, here],
+            src_ref=above_ref.at[1 - side, :, pl.ds(to * share, share)],
+            dst_ref=other_ref.at[pair],
+            send_sem=w_send.at[to],
+            recv_sem=w_recv.at[pair],
+            device_id={"blk": r, "box": 2 * to + 1 - side},
+            device_id_type=MESH,
+        )
+
+    for to in range(pairs):
+        send_w(to).start()
+
+    for copy in pair_copies:
+        copy.wait_recv()
+    top = split(
+        jnp.concatenate(
+            [
+                jnp.concatenate([g_ref[i, 0], g_ref[i, 1]], axis=1)
+                for i in range(2)
+            ],
+            axis=0,
+        )
+    )
+    none = jnp.zeros((rank, width), F32)
+    spread = split(
+        jnp.concatenate(
+            [
+                jnp.concatenate([p_ref[0, c], none] if i == 0 else [none, p_ref[1, c]], axis=1)
+                for c in range(2)
+                for i in range(2)
+            ],
+            axis=0,
+        )
+    )
+
+    for d in range(1, n_box):
+        send_t(0, d).wait_recv()
+    y = dot3(top, both(t_ref[...].reshape(n_box * rank, count)))
+    x = dot3(both_transposed(y), spread)
+    x_ref[0] = above_ref[side] + x[:, :width].reshape(2, half, width)
+    x_ref[1] = x[:, width:].reshape(2, half, width)
+
+    def send_x(to, here):
+        return pltpu.make_async_remote_copy(
+            src_ref=x_ref.at[:, :, pl.ds(to * share, share)],
+            dst_ref=came_ref.at[here],
             send_sem=x_send.at[to],
-            recv_sem=x_recv.at[d],
-            device_id={"blk": r, "box": to},
+            recv_sem=x_recv.at[here],
+            device_id={"blk": r, "box": 2 * to + side},
             device_id_type=MESH,
         )
 
-    for h in range(2):
-        for copy in t_copies[h]:
-            copy.wait_recv()
-        y = dot3(top, both(t_ref[h].reshape(n_box * rank, count)))
-        x_ref[h] = (x[h] + dot3(both_transposed(y), picked_below)).reshape(2, half, width)
-        for to in range(h * places, h * places + places):
-
-            @pl.when(q != to)
-            def _(to=to):
-                send_x(to).start()
-
-    start = pl.multiple_of(lax.rem(q, places) * share, share)
-    out_ref[:, :, here] = x_ref[q // places, :, pl.ds(start, share)]
-
-    for d in range(1, n_box):
+    for to in range(pairs):
+
+        @pl.when(pair != to)
+        def _(to=to):
+            send_x(to, pair).start()
+
+    def place(box):
+        return pl.ds(pl.multiple_of(box * width, width), width)
+
+    for here in range(pairs):
         pltpu.make_async_remote_copy(
-            src_ref=x_ref.at[0, :, pl.ds(0, share)],
-            dst_ref=out_ref.at[:, :, pl.ds(pl.multiple_of(lax.rem(q - d + n_box, n_box) * width, width), width)],
-            send_sem=x_send.at[0],
-            recv_sem=x_recv.at[d],
-            device_id=around(0, d),
+            src_ref=above_ref.at[0, :, pl.ds(0, share)],
+            dst_ref=other_ref.at[here],
+            send_sem=w_send.at[here],
+            recv_sem=w_recv.at[here],
+            device_id=across(1),
             device_id_type=MESH,
         ).wait_recv()
-    for copy in u_copies[0] + u_copies[1] + t_copies[0] + t_copies[1]:
+
+    own = pl.ds(pl.multiple_of(pair * share, share), share)
+    out_ref[:, :, place(q)] = x_ref[0, :, own]
+    out_ref[:, :, place(2 * pair + 1 - side)] = x_ref[1, :, own] + other_ref[pair]
+
+    for here in range(pairs):
+
+        @pl.when(pair != here)
+        def _(here=here):
+            send_x(here, here).wait_recv()
+            out_ref[:, :, place(2 * here + side)] = came_ref[here, 0]
+            out_ref[:, :, place(2 * here + 1 - side)] = came_ref[here, 1] + other_ref[here]
+
+    for copy in u_copies[0] + u_copies[1] + pair_copies:
         copy.wait_send()
-    for to in range(n_box):
-
-        @pl.when(q != to)
+    for d in range(1, n_box):
+        send_t(0, d).wait_send()
+    for to in range(pairs):
+        send_w(to).wait_send()
+
+        @pl.when(pair != to)
         def _(to=to):
-            send_x(to).wait_send()
+            send_x(to, pair).wait_send()
 
 
 def on_device(
@@ -294,18 +384,27 @@
             pltpu.SMEM(skeleton.shape, jnp.int32),
             pltpu.VMEM(box_inverse_parts.shape[1:], F32),
             pltpu.VMEM(near_coupling.shape[1:], F32),
-            pltpu.VMEM(top_inverse.shape[1:], F32),
+            pltpu.VMEM((2, *top_inverse.shape[1:]), F32),
             pltpu.VMEM((2, rank, count), F32),
             pltpu.VMEM((2, len(OFFSETS), rank, count), F32),
-            pltpu.VMEM((2, n_box, rank, count), F32),
+            pltpu.VMEM((2, rank, count), F32),
+            pltpu.VMEM((n_box, rank, count), F32),
+            pltpu.VMEM((2, 2, rank, width), F32),
             pltpu.VMEM((2, 2, count // 2, width), F32),
+            pltpu.VMEM((n_box // 2, 2, count // n_box, width), F32),
+            pltpu.VMEM((2, 2, count // 2, width), F32),
+            pltpu.VMEM((n_box // 2, 2, 2, count // n_box, width), F32),
             pltpu.SemaphoreType.DMA((7,)),
             pltpu.SemaphoreType.DMA((2, len(OFFSETS))),
             pltpu.SemaphoreType.DMA((2, len(OFFSETS))),
-            pltpu.SemaphoreType.DMA((2, n_box)),
-            pltpu.SemaphoreType.DMA((2, n_box)),
             pltpu.SemaphoreType.DMA((n_box,)),
             pltpu.SemaphoreType.DMA((n_box,)),
+            pltpu.SemaphoreType.DMA((2,)),
+            pltpu.SemaphoreType.DMA((2,)),
+            pltpu.SemaphoreType.DMA((n_box // 2,)),
+            pltpu.SemaphoreType.DMA((n_box // 2,)),
+            pltpu.SemaphoreType.DMA((n_box // 2,)),
+            pltpu.SemaphoreType.DMA((n_box // 2,)),
         ],
         compiler_params=pltpu.CompilerParams(
             collective_id=0, has_side_effects=True, vmem_limit_bytes=16 * 1024 * 1024

time: 24.1 us -> 22.2 us (0.921)
  Pallas kernels: 23.2 us -> 21.3 us
    pallas_call x1, Pallas kernels: 23.2 us -> 21.3 us  [on_device(): pl.pallas_call(functools.partial(kernel, n_blk, n_box), out_shape=jax.Sha...]
where the time goes in v3:
time: 22.2 us; the launch traced here: 22 us
  Pallas kernels  21.3 us (96%)
  local copies, waits for them, and re-layouts  0.66 us (3%)
    pallas_call x1, Pallas kernels, on_device(): pl.pallas_call(functools.partial(kernel, n_blk, n_box), out_shape=jax.Sha...  21.3 us
    unnamed x1, local copies, waits for them, and re-layouts  0.66 us

profile of v3, /device:TPU:0, one launch (start us, length us, event | category | flops | bytes accessed | tf_op | source)
XLA Modules:
  0.0 22.0 jit_solution(9375764735833028929)
XLA Ops:
  0.0 21.3 %shard_map.73 = f32[2,16,1024]{2,1,0:T(8,128)S(1)} custom-call(f32[3,128]{1,0:T(4,128)} %points_hbm.1, s32[1,128]{1,0:T(1,128)} %bitcast.1, s32[1,8]{1,0:T(1,128)} %mask_hbm.1, s32[1,32]{1,0:T(1,128)} %skeleton_hbm.1, f32[1,2,128,128]{3,2,1,0:T(8,128)} %l_hbm.1, f32[1,8,2,32,128]{4,3,2,1,0:T(8,128)} %e_hbm.1, f32[1,2,32,256]{3,2,1,0:T(8,128)} %g_hbm.1), custom_call_target="tpu_custom_call" | custom-call | tf_op jit(solution)/shard_map/pallas_call | solution.py:375
  21.4 0.7 %copy.9 = f32[2,16,1024]{2,1,0:T(8,128)} copy(f32[2,16,1024]{2,1,0:T(8,128)S(1)} %shard_map.73) | data formatting | bytes 262144

commit v4 on v3

--- a/solution.py
+++ b/solution.py
@@ -41,12 +41,32 @@
     return jnp.dot(a, b, preferred_element_type=F32)
 
 
-def dot3(a, b):
-    return dot(a[0], b[0]) + (dot(a[0], b[1]) + dot(a[1], b[0]))
-
-
-def beside(a, b, axis):
-    return tuple(jnp.concatenate([a[i], b[i]], axis=axis) for i in range(2))
+def stacked(*parts):
+    return split(jnp.concatenate(parts, axis=0))
+
+
+def tall(a):
+    return jnp.concatenate(a, axis=0)
+
+
+def wide(b):
+    return jnp.concatenate(b, axis=1)
+
+
+def product(a, b):
+    m, n = a.shape[0] // 2, b.shape[1] // 2
+    c = dot(a, b)
+    return c[:m, :n] + (c[:m, n:] + c[m:, :n])
+
+
+def deep_left(a):
+    high, low = split(a)
+    return jnp.concatenate([high, low, high], axis=1)
+
+
+def deep_right(b):
+    high, low = split(b)
+    return jnp.concatenate([high, high, low], axis=0)
 
 
 def kernel(
@@ -155,15 +175,17 @@
     def turned(a):
         return jnp.where(first, -1.0, 1.0) * pltpu.roll(a, half, 1)
 
-    def both(a):
-        return split(jnp.concatenate([a, turned(a)], axis=0))
-
-    def both_transposed(a):
-        return split(jnp.concatenate([a.T, turned(a).T], axis=1))
+    def complex_of(a):
+        m = a.shape[0] // 2
+        return a[:m] + turned(a[m:])
+
+    def transposed_of(a):
+        re, im = a[:, :width], a[:, width:]
+        return jnp.stack([re[:half] - im[half:], re[half:] + im[:half]])
 
     field = [
-        both(jnp.where(first, cosine, pltpu.roll(sine, half, 1))),
-        both(jnp.where(first, pltpu.roll(cosine, half, 1), sine)),
+        wide(split(jnp.where(first, cosine, pltpu.roll(sine, half, 1)))),
+        wide(split(jnp.where(first, pltpu.roll(cosine, half, 1), sine))),
     ]
 
     loads[4].wait()
@@ -175,13 +197,13 @@
     picker = jnp.where(wanted == lane, 1.0, 0.0).astype(BF16)
 
     def pick(a):
-        return tuple(dot(picker, half).astype(BF16) for half in a)
+        return tuple(dot(picker, part).astype(BF16) for part in a)
 
     loads[2].wait()
     lr, li = split(l_ref[0]), split(l_ref[1])
     plr, pli = pick(lr), pick(li)
-    picked = beside(plr, pli, 1)
-    u = [dot3(picked, part) for part in field]
+    picked = tall([plr[0], pli[0], plr[1], pli[1]])
+    u = [complex_of(product(picked, part)) for part in field]
     for h in range(2):
         u_ref[h] = u[h]
     for i, part in enumerate((plr, pli)):
@@ -218,8 +240,8 @@
     for copy in pair_copies:
         copy.start()
 
-    whole = beside(lr, li, 1)
-    z = [dot3(whole, part) for part in field]
+    whole = tall([lr[0], li[0], lr[1], li[1]])
+    z = [complex_of(product(whole, part)) for part in field]
     loads[3].wait()
     loads[5].wait()
     masked = [
@@ -227,8 +249,9 @@
     ]
     er = split(jnp.concatenate([e[0] for e in masked], axis=0).T)
     ei = split(jnp.concatenate([e[1] for e in masked], axis=0).T)
-    coupling = beside(er, ei, 1)
-    picked_coupling = beside(pick(er), pick(ei), 1)
+    per, pei = pick(er), pick(ei)
+    coupling = tall([er[0], ei[0], er[1], ei[1]])
+    picked_coupling = tall([per[0], pei[0], per[1], pei[1]])
 
     def send_t(h, d):
         return pltpu.make_async_remote_copy(
@@ -244,9 +267,9 @@
     for h in range(2):
         for copy in u_copies[h]:
             copy.wait_recv()
-        near.append(both(near_ref[h].reshape(len(OFFSETS) * rank, count)))
-        mine_ref[h] = u[h] - dot3(picked_coupling, near[h])
-        for d in range(1, n_box):
+        near.append(wide(split(near_ref[h].reshape(len(OFFSETS) * rank, count))))
+        mine_ref[h] = u[h] - complex_of(product(picked_coupling, near[h]))
+        for d in sorted(range(1, n_box), key=lambda d: -d.bit_length()):
 
             @pl.when(lax.rem(q + d, 2) == h)
             def _(h=h, d=d):
@@ -254,11 +277,10 @@
 
     t_ref[pl.ds(q, 1)] = mine_ref[pl.ds(side, 1)]
 
-    below = beside(lr, li, 0)
+    below = deep_right(jnp.concatenate([l_ref[0], l_ref[1]], axis=1))
     for h in range(2):
-        above_ref[h] = dot3(
-            both_transposed(z[h] - dot3(coupling, near[h])), below
-        ).reshape(2, half, width)
+        w = z[h] - complex_of(product(coupling, near[h]))
+        above_ref[h] = transposed_of(dot(deep_left(w.T), below))
 
     def send_w(to):
         return pltpu.make_async_remote_copy(
@@ -275,33 +297,24 @@
 
     for copy in pair_copies:
         copy.wait_recv()
-    top = split(
+    top = tall(stacked(g_ref[0, 0], g_ref[1, 0], g_ref[0, 1], g_ref[1, 1]))
+    none = jnp.zeros((rank, width), F32)
+    spread = deep_right(
         jnp.concatenate(
             [
-                jnp.concatenate([g_ref[i, 0], g_ref[i, 1]], axis=1)
-                for i in range(2)
+                jnp.concatenate([p_ref[0, 0], p_ref[0, 1], none, none], axis=1),
+                jnp.concatenate([none, none, p_ref[1, 0], p_ref[1, 1]], axis=1),
             ],
             axis=0,
         )
     )
-    none = jnp.zeros((rank, width), F32)
-    spread = split(
-        jnp.concatenate(
-            [
-                jnp.concatenate([p_ref[0, c], none] if i == 0 else [none, p_ref[1, c]], axis=1)
-                for c in range(2)
-                for i in range(2)
-            ],
-            axis=0,
-        )
-    )
 
     for d in range(1, n_box):
         send_t(0, d).wait_recv()
-    y = dot3(top, both(t_ref[...].reshape(n_box * rank, count)))
-    x = dot3(both_transposed(y), spread)
-    x_ref[0] = above_ref[side] + x[:, :width].reshape(2, half, width)
-    x_ref[1] = x[:, width:].reshape(2, half, width)
+    y = complex_of(product(top, wide(split(t_ref[...].reshape(n_box * rank, count)))))
+    x = dot(deep_left(y.T), spread)
+    x_ref[0] = above_ref[side] + transposed_of(x[:, : 2 * width])
+    x_ref[1] = transposed_of(x[:, 2 * width :])
 
     def send_x(to, here):
         return pltpu.make_async_remote_copy(

time: 22.2 us -> 21.8 us (0.982)
  Pallas kernels: 21.3 us -> 21 us
    pallas_call x1, Pallas kernels: 21.3 us -> 21 us  [on_device(): pl.pallas_call(functools.partial(kernel, n_blk, n_box), out_shape=jax.Sha...]
where the time goes in v4:
time: 21.8 us; the launch traced here: 21.7 us
  Pallas kernels  21 us (96%)
  local copies, waits for them, and re-layouts  0.66 us (3%)
    pallas_call x1, Pallas kernels, on_device(): pl.pallas_call(functools.partial(kernel, n_blk, n_box), out_shape=jax.Sha...  21 us
    unnamed x1, local copies, waits for them, and re-layouts  0.66 us

profile of v4, /device:TPU:0, one launch (start us, length us, event | category | flops | bytes accessed | tf_op | source)
XLA Modules:
  0.0 21.7 jit_solution(18316431356739282526)
XLA Ops:
  0.0 21.0 %shard_map.73 = f32[2,16,1024]{2,1,0:T(8,128)S(1)} custom-call(f32[3,128]{1,0:T(4,128)} %points_hbm.1, s32[1,128]{1,0:T(1,128)} %bitcast.1, s32[1,8]{1,0:T(1,128)} %mask_hbm.1, s32[1,32]{1,0:T(1,128)} %skeleton_hbm.1, f32[1,2,128,128]{3,2,1,0:T(8,128)} %l_hbm.1, f32[1,8,2,32,128]{4,3,2,1,0:T(8,128)} %e_hbm.1, f32[1,2,32,256]{3,2,1,0:T(8,128)} %g_hbm.1), custom_call_target="tpu_custom_call" | custom-call | tf_op jit(solution)/shard_map/pallas_call | solution.py:388
  21.0 0.7 %copy.9 = f32[2,16,1024]{2,1,0:T(8,128)} copy(f32[2,16,1024]{2,1,0:T(8,128)S(1)} %shard_map.73) | data formatting | bytes 262144

commit v5 on v4

--- a/solution.py
+++ b/solution.py
@@ -96,6 +96,7 @@
     other_ref,
     x_ref,
     came_ref,
+    held_ref,
     load_sem,
     u_send,
     u_recv,
@@ -103,6 +104,8 @@
     t_recv,
     pair_send,
     pair_recv,
+    own_send,
+    own_recv,
     w_send,
     w_recv,
     x_send,
@@ -118,6 +121,8 @@
     pairs = n_box // 2
     pair = q // 2
     side = lax.rem(q, 2)
+    mate = r + 1 - 2 * lax.rem(r, 2)
+    beyond = lax.rem(r - 1 + 2 * lax.rem(r, 2) + n_blk, n_blk)
 
     def around(dr, dq):
         return {"blk": lax.rem(r + dr + n_blk, n_blk), "box": lax.rem(q + dq + n_box, n_box)}
@@ -129,7 +134,7 @@
             if k & bit:
                 place = place + bit - 2 * bit * lax.rem(q // bit, 2)
             bit *= 2
-        return {"blk": r, "box": place}
+        return {"blk": mate, "box": place}
 
     loads = [
         pltpu.make_async_copy(angles_hbm, angles_ref, load_sem.at[0]),
@@ -145,7 +150,8 @@
 
     barrier = pltpu.get_barrier_semaphore()
     greeted = [around(0, d) for d in range(1, n_box)]
-    greeted += [around(dr, dq) for dr, dq in OFFSETS if dr != 0]
+    greeted += [{"blk": mate, "box": to} for to in range(n_box)]
+    greeted += [{"blk": beyond, "box": around(0, dq)["box"]} for dq in (-1, 0, 1)]
     for device in greeted:
         pl.semaphore_signal(barrier, inc=1, device_id=device, device_id_type=MESH)
 
@@ -228,12 +234,13 @@
     pair_copies = [
         pltpu.make_async_remote_copy(
             src_ref=ref.at[0],
-            dst_ref=ref.at[1],
-            send_sem=pair_send.at[i],
-            recv_sem=pair_recv.at[i],
-            device_id=across(1),
+            dst_ref=ref.at[1 + d],
+            send_sem=pair_send.at[i, d],
+            recv_sem=pair_recv.at[i, d],
+            device_id=across(d),
             device_id_type=MESH,
         )
+        for d in (1, 0)
         for i, ref in enumerate((g_ref, p_ref))
     ]
     loads[6].wait()
@@ -269,13 +276,11 @@
             copy.wait_recv()
         near.append(wide(split(near_ref[h].reshape(len(OFFSETS) * rank, count))))
         mine_ref[h] = u[h] - complex_of(product(picked_coupling, near[h]))
-        for d in sorted(range(1, n_box), key=lambda d: -d.bit_length()):
+        for d in sorted(range(n_box), key=lambda d: -d.bit_length()):
 
             @pl.when(lax.rem(q + d, 2) == h)
             def _(h=h, d=d):
                 send_t(h, d).start()
-
-    t_ref[pl.ds(q, 1)] = mine_ref[pl.ds(side, 1)]
 
     below = deep_right(jnp.concatenate([l_ref[0], l_ref[1]], axis=1))
     for h in range(2):
@@ -292,28 +297,38 @@
             device_id_type=MESH,
         )
 
+    own_half = pltpu.make_async_remote_copy(
+        src_ref=above_ref.at[side],
+        dst_ref=held_ref,
+        send_sem=own_send,
+        recv_sem=own_recv,
+        device_id=across(0),
+        device_id_type=MESH,
+    )
+    own_half.start()
     for to in range(pairs):
         send_w(to).start()
 
     for copy in pair_copies:
         copy.wait_recv()
-    top = tall(stacked(g_ref[0, 0], g_ref[1, 0], g_ref[0, 1], g_ref[1, 1]))
+    top = tall(stacked(g_ref[1, 0], g_ref[2, 0], g_ref[1, 1], g_ref[2, 1]))
     none = jnp.zeros((rank, width), F32)
     spread = deep_right(
         jnp.concatenate(
             [
-                jnp.concatenate([p_ref[0, 0], p_ref[0, 1], none, none], axis=1),
-                jnp.concatenate([none, none, p_ref[1, 0], p_ref[1, 1]], axis=1),
+                jnp.concatenate([p_ref[1, 0], p_ref[1, 1], none, none], axis=1),
+                jnp.concatenate([none, none, p_ref[2, 0], p_ref[2, 1]], axis=1),
             ],
             axis=0,
         )
     )
 
-    for d in range(1, n_box):
+    own_half.wait_recv()
+    for d in range(n_box):
         send_t(0, d).wait_recv()
     y = complex_of(product(top, wide(split(t_ref[...].reshape(n_box * rank, count)))))
     x = dot(deep_left(y.T), spread)
-    x_ref[0] = above_ref[side] + transposed_of(x[:, : 2 * width])
+    x_ref[0] = held_ref[...] + transposed_of(x[:, : 2 * width])
     x_ref[1] = transposed_of(x[:, 2 * width :])
 
     def send_x(to, here):
@@ -322,15 +337,12 @@
             dst_ref=came_ref.at[here],
             send_sem=x_send.at[to],
             recv_sem=x_recv.at[here],
-            device_id={"blk": r, "box": 2 * to + side},
+            device_id={"blk": mate, "box": 2 * to + side},
             device_id_type=MESH,
         )
 
     for to in range(pairs):
-
-        @pl.when(pair != to)
-        def _(to=to):
-            send_x(to, pair).start()
+        send_x(to, pair).start()
 
     def place(box):
         return pl.ds(pl.multiple_of(box * width, width), width)
@@ -345,28 +357,19 @@
             device_id_type=MESH,
         ).wait_recv()
 
-    own = pl.ds(pl.multiple_of(pair * share, share), share)
-    out_ref[:, :, place(q)] = x_ref[0, :, own]
-    out_ref[:, :, place(2 * pair + 1 - side)] = x_ref[1, :, own] + other_ref[pair]
-
     for here in range(pairs):
-
-        @pl.when(pair != here)
-        def _(here=here):
-            send_x(here, here).wait_recv()
-            out_ref[:, :, place(2 * here + side)] = came_ref[here, 0]
-            out_ref[:, :, place(2 * here + 1 - side)] = came_ref[here, 1] + other_ref[here]
+        send_x(here, here).wait_recv()
+        out_ref[:, :, place(2 * here + side)] = came_ref[here, 0]
+        out_ref[:, :, place(2 * here + 1 - side)] = came_ref[here, 1] + other_ref[here]
 
     for copy in u_copies[0] + u_copies[1] + pair_copies:
         copy.wait_send()
-    for d in range(1, n_box):
+    own_half.wait_send()
+    for d in range(n_box):
         send_t(0, d).wait_send()
     for to in range(pairs):
         send_w(to).wait_send()
-
-        @pl.when(pair != to)
-        def _(to=to):
-            send_x(to, pair).wait_send()
+        send_x(to, pair).wait_send()
 
 
 def on_device(
@@ -397,23 +400,26 @@
             pltpu.SMEM(skeleton.shape, jnp.int32),
             pltpu.VMEM(box_inverse_parts.shape[1:], F32),
             pltpu.VMEM(near_coupling.shape[1:], F32),
-            pltpu.VMEM((2, *top_inverse.shape[1:]), F32),
+            pltpu.VMEM((3, *top_inverse.shape[1:]), F32),
             pltpu.VMEM((2, rank, count), F32),
             pltpu.VMEM((2, len(OFFSETS), rank, count), F32),
             pltpu.VMEM((2, rank, count), F32),
             pltpu.VMEM((n_box, rank, count), F32),
-            pltpu.VMEM((2, 2, rank, width), F32),
+            pltpu.VMEM((3, 2, rank, width), F32),
             pltpu.VMEM((2, 2, count // 2, width), F32),
             pltpu.VMEM((n_box // 2, 2, count // n_box, width), F32),
             pltpu.VMEM((2, 2, count // 2, width), F32),
             pltpu.VMEM((n_box // 2, 2, 2, count // n_box, width), F32),
+            pltpu.VMEM((2, count // 2, width), F32),
             pltpu.SemaphoreType.DMA((7,)),
             pltpu.SemaphoreType.DMA((2, len(OFFSETS))),
             pltpu.SemaphoreType.DMA((2, len(OFFSETS))),
             pltpu.SemaphoreType.DMA((n_box,)),
             pltpu.SemaphoreType.DMA((n_box,)),
-            pltpu.SemaphoreType.DMA((2,)),
-            pltpu.SemaphoreType.DMA((2,)),
+            pltpu.SemaphoreType.DMA((2, 2)),
+            pltpu.SemaphoreType.DMA((2, 2)),
+            pltpu.SemaphoreType.DMA,
+            pltpu.SemaphoreType.DMA,
             pltpu.SemaphoreType.DMA((n_box // 2,)),
             pltpu.SemaphoreType.DMA((n_box // 2,)),
             pltpu.SemaphoreType.DMA((n_box // 2,)),

time: 21.8 us -> 21.5 us (0.986)
  Pallas kernels: 21 us -> 20.7 us
    pallas_call x1, Pallas kernels: 21 us -> 20.7 us  [on_device(): pl.pallas_call(functools.partial(kernel, n_blk, n_box), out_shape=jax.Sha...]
where the time goes in v5:
time: 21.5 us; the launch traced here: 21.4 us
  Pallas kernels  20.7 us (96%)
  local copies, waits for them, and re-layouts  0.66 us (3%)
    pallas_call x1, Pallas kernels, on_device(): pl.pallas_call(functools.partial(kernel, n_blk, n_box), out_shape=jax.Sha...  20.7 us
    unnamed x1, local copies, waits for them, and re-layouts  0.66 us

profile of v5, /device:TPU:0, one launch (start us, length us, event | category | flops | bytes accessed | tf_op | source)
XLA Modules:
  0.0 21.4 jit_solution(10497347731193930778)
XLA Ops:
  0.0 20.7 %shard_map.73 = f32[2,16,1024]{2,1,0:T(8,128)S(1)} custom-call(f32[3,128]{1,0:T(4,128)} %points_hbm.1, s32[1,128]{1,0:T(1,128)} %bitcast.1, s32[1,8]{1,0:T(1,128)} %mask_hbm.1, s32[1,32]{1,0:T(1,128)} %skeleton_hbm.1, f32[1,2,128,128]{3,2,1,0:T(8,128)} %l_hbm.1, f32[1,8,2,32,128]{4,3,2,1,0:T(8,128)} %e_hbm.1, f32[1,2,32,256]{3,2,1,0:T(8,128)} %g_hbm.1), custom_call_target="tpu_custom_call" | custom-call | tf_op jit(solution)/shard_map/pallas_call | solution.py:391
  20.7 0.7 %copy.9 = f32[2,16,1024]{2,1,0:T(8,128)} copy(f32[2,16,1024]{2,1,0:T(8,128)S(1)} %shard_map.73) | data formatting | bytes 262144

commit v6 on v5

--- a/solution.py
+++ b/solution.py
@@ -39,10 +39,6 @@
 
 def dot(a, b):
     return jnp.dot(a, b, preferred_element_type=F32)
-
-
-def stacked(*parts):
-    return split(jnp.concatenate(parts, axis=0))
 
 
 def tall(a):
@@ -97,6 +93,7 @@
     x_ref,
     came_ref,
     held_ref,
+    joined_ref,
     load_sem,
     u_send,
     u_recv,
@@ -311,23 +308,40 @@
 
     for copy in pair_copies:
         copy.wait_recv()
-    top = tall(stacked(g_ref[1, 0], g_ref[2, 0], g_ref[1, 1], g_ref[2, 1]))
-    none = jnp.zeros((rank, width), F32)
-    spread = deep_right(
-        jnp.concatenate(
-            [
-                jnp.concatenate([p_ref[1, 0], p_ref[1, 1], none, none], axis=1),
-                jnp.concatenate([none, none, p_ref[2, 0], p_ref[2, 1]], axis=1),
-            ],
-            axis=0,
-        )
+    joined = jnp.concatenate(
+        [
+            dot(
+                deep_left(jnp.concatenate([g_ref[i, 0], g_ref[i, 1]], axis=0).T),
+                deep_right(
+                    jnp.concatenate(
+                        [
+                            jnp.concatenate([p_ref[i, 0], p_ref[i, 1]], axis=1),
+                            jnp.concatenate([-p_ref[i, 1], p_ref[i, 0]], axis=1),
+                        ],
+                        axis=0,
+                    )
+                ),
+            )
+            for i in (1, 2)
+        ],
+        axis=1,
     )
-
+    depth = pairs * rank
+    for g in range(2):
+        joined_ref[g] = deep_right(joined[g * depth : (g + 1) * depth])
+
+    def part_of_x(g):
+        t = t_ref[pl.ds(g * pairs, pairs)].reshape(depth, count)
+        return dot(deep_left(t.T), joined_ref[g])
+
+    near_half = q // pairs
+    for d in range(pairs):
+        send_t(0, d).wait_recv()
+    x = part_of_x(near_half)
     own_half.wait_recv()
-    for d in range(n_box):
+    for d in range(pairs, n_box):
         send_t(0, d).wait_recv()
-    y = complex_of(product(top, wide(split(t_ref[...].reshape(n_box * rank, count)))))
-    x = dot(deep_left(y.T), spread)
+    x = x + part_of_x(1 - near_half)
     x_ref[0] = held_ref[...] + transposed_of(x[:, : 2 * width])
     x_ref[1] = transposed_of(x[:, 2 * width :])
 
@@ -411,6 +425,7 @@
             pltpu.VMEM((2, 2, count // 2, width), F32),
             pltpu.VMEM((n_box // 2, 2, 2, count // n_box, width), F32),
             pltpu.VMEM((2, count // 2, width), F32),
+            pltpu.VMEM((2, 3 * n_box // 2 * rank, 4 * width), BF16),
             pltpu.SemaphoreType.DMA((7,)),
             pltpu.SemaphoreType.DMA((2, len(OFFSETS))),
             pltpu.SemaphoreType.DMA((2, len(OFFSETS))),

time: 21.5 us -> 21.2 us (0.986)
  Pallas kernels: 20.7 us -> 20.4 us
    pallas_call x1, Pallas kernels: 20.7 us -> 20.4 us  [on_device(): pl.pallas_call(functools.partial(kernel, n_blk, n_box), out_shape=jax.Sha...]
where the time goes in v6:
time: 21.2 us; the launch traced here: 21.1 us
  Pallas kernels  20.4 us (96%)
  local copies, waits for them, and re-layouts  0.66 us (3%)
    pallas_call x1, Pallas kernels, on_device(): pl.pallas_call(functools.partial(kernel, n_blk, n_box), out_shape=jax.Sha...  20.4 us
    unnamed x1, local copies, waits for them, and re-layouts  0.66 us

profile of v6, /device:TPU:0, one launch (start us, length us, event | category | flops | bytes accessed | tf_op | source)
XLA Modules:
  0.0 21.1 jit_solution(18119286115495287020)
XLA Ops:
  0.0 20.4 %shard_map.73 = f32[2,16,1024]{2,1,0:T(8,128)S(1)} custom-call(f32[3,128]{1,0:T(4,128)} %points_hbm.1, s32[1,128]{1,0:T(1,128)} %bitcast.1, s32[1,8]{1,0:T(1,128)} %mask_hbm.1, s32[1,32]{1,0:T(1,128)} %skeleton_hbm.1, f32[1,2,128,128]{3,2,1,0:T(8,128)} %l_hbm.1, f32[1,8,2,32,128]{4,3,2,1,0:T(8,128)} %e_hbm.1, f32[1,2,32,256]{3,2,1,0:T(8,128)} %g_hbm.1), custom_call_target="tpu_custom_call" | custom-call | tf_op jit(solution)/shard_map/pallas_call | solution.py:405
  20.4 0.7 %copy.9 = f32[2,16,1024]{2,1,0:T(8,128)} copy(f32[2,16,1024]{2,1,0:T(8,128)S(1)} %shard_map.73) | data formatting | bytes 262144

commit v7 on v6

--- a/solution.py
+++ b/solution.py
@@ -273,7 +273,7 @@
             copy.wait_recv()
         near.append(wide(split(near_ref[h].reshape(len(OFFSETS) * rank, count))))
         mine_ref[h] = u[h] - complex_of(product(picked_coupling, near[h]))
-        for d in sorted(range(n_box), key=lambda d: -d.bit_length()):
+        for d in (*sorted(range(2, n_box, 2), key=lambda d: (d.bit_count(), -d)), *range(n_box - 1, 0, -2), 0):
 
             @pl.when(lax.rem(q + d, 2) == h)
             def _(h=h, d=d):
@@ -355,7 +355,7 @@
             device_id_type=MESH,
         )
 
-    for to in range(pairs):
+    for to in (0, *range(pairs - 1, 0, -1)):
         send_x(to, pair).start()
 
     def place(box):

time: 21.2 us -> 21.1 us (level)
  Pallas kernels: 20.4 us -> 20.1 us
    pallas_call x1, Pallas kernels: 20.4 us -> 20.1 us  [on_device(): pl.pallas_call(functools.partial(kernel, n_blk, n_box), out_shape=jax.Sha...]
where the time goes in v7:
time: 21.1 us; the launch traced here: 20.8 us
  Pallas kernels  20.1 us (95%)
  local copies, waits for them, and re-layouts  0.66 us (3%)
    pallas_call x1, Pallas kernels, on_device(): pl.pallas_call(functools.partial(kernel, n_blk, n_box), out_shape=jax.Sha...  20.1 us
    unnamed x1, local copies, waits for them, and re-layouts  0.66 us

profile of v7, /device:TPU:0, one launch (start us, length us, event | category | flops | bytes accessed | tf_op | source)
XLA Modules:
  0.0 20.8 jit_solution(2281291149239113735)
XLA Ops:
  0.0 20.1 %shard_map.73 = f32[2,16,1024]{2,1,0:T(8,128)S(1)} custom-call(f32[3,128]{1,0:T(4,128)} %points_hbm.1, s32[1,128]{1,0:T(1,128)} %bitcast.1, s32[1,8]{1,0:T(1,128)} %mask_hbm.1, s32[1,32]{1,0:T(1,128)} %skeleton_hbm.1, f32[1,2,128,128]{3,2,1,0:T(8,128)} %l_hbm.1, f32[1,8,2,32,128]{4,3,2,1,0:T(8,128)} %e_hbm.1, f32[1,2,32,256]{3,2,1,0:T(8,128)} %g_hbm.1), custom_call_target="tpu_custom_call" | custom-call | tf_op jit(solution)/shard_map/pallas_call | solution.py:405
  20.1 0.7 %copy.9 = f32[2,16,1024]{2,1,0:T(8,128)} copy(f32[2,16,1024]{2,1,0:T(8,128)S(1)} %shard_map.73) | data formatting | bytes 262144

commit v8 on v7

--- a/solution.py
+++ b/solution.py
@@ -140,7 +140,6 @@
         pltpu.make_async_copy(e_hbm.at[0], e_ref, load_sem.at[3]),
         pltpu.make_async_copy(skeleton_hbm, skeleton_ref, load_sem.at[5]),
         pltpu.make_async_copy(mask_hbm, mask_ref, load_sem.at[6]),
-        pltpu.make_async_copy(g_hbm.at[0], g_ref.at[0], load_sem.at[4]),
     ]
     for load in loads:
         load.start()
@@ -230,7 +229,7 @@
 
     pair_copies = [
         pltpu.make_async_remote_copy(
-            src_ref=ref.at[0],
+            src_ref=source,
             dst_ref=ref.at[1 + d],
             send_sem=pair_send.at[i, d],
             recv_sem=pair_recv.at[i, d],
@@ -238,9 +237,8 @@
             device_id_type=MESH,
         )
         for d in (1, 0)
-        for i, ref in enumerate((g_ref, p_ref))
+        for i, (source, ref) in enumerate(((g_hbm.at[0], g_ref), (p_ref.at[0], p_ref)))
     ]
-    loads[6].wait()
     for copy in pair_copies:
         copy.start()
 

time: 21.1 us -> 21.7 us (1.028)
  Pallas kernels: 20.1 us -> 20.9 us
    pallas_call x1, Pallas kernels: 20.1 us -> 20.9 us  [on_device(): pl.pallas_call(functools.partial(kernel, n_blk, n_box), out_shape=jax.Sha...]
where the time goes in v8:
time: 21.7 us; the launch traced here: 21.6 us
  Pallas kernels  20.9 us (96%)
  local copies, waits for them, and re-layouts  0.66 us (3%)
    pallas_call x1, Pallas kernels, on_device(): pl.pallas_call(functools.partial(kernel, n_blk, n_box), out_shape=jax.Sha...  20.9 us
    unnamed x1, local copies, waits for them, and re-layouts  0.66 us

profile of v8, /device:TPU:0, one launch (start us, length us, event | category | flops | bytes accessed | tf_op | source)
XLA Modules:
  0.0 21.6 jit_solution(7942474770850124078)
XLA Ops:
  0.0 20.9 %shard_map.73 = f32[2,16,1024]{2,1,0:T(8,128)S(1)} custom-call(f32[3,128]{1,0:T(4,128)} %points_hbm.1, s32[1,128]{1,0:T(1,128)} %bitcast.1, s32[1,8]{1,0:T(1,128)} %mask_hbm.1, s32[1,32]{1,0:T(1,128)} %skeleton_hbm.1, f32[1,2,128,128]{3,2,1,0:T(8,128)} %l_hbm.1, f32[1,8,2,32,128]{4,3,2,1,0:T(8,128)} %e_hbm.1, f32[1,2,32,256]{3,2,1,0:T(8,128)} %g_hbm.1), custom_call_target="tpu_custom_call" | custom-call | tf_op jit(solution)/shard_map/pallas_call | solution.py:403
  20.9 0.7 %copy.9 = f32[2,16,1024]{2,1,0:T(8,128)} copy(f32[2,16,1024]{2,1,0:T(8,128)S(1)} %shard_map.73) | data formatting | bytes 262144

commit v9 on v7

--- a/solution.py
+++ b/solution.py
@@ -273,11 +273,15 @@
             copy.wait_recv()
         near.append(wide(split(near_ref[h].reshape(len(OFFSETS) * rank, count))))
         mine_ref[h] = u[h] - complex_of(product(picked_coupling, near[h]))
-        for d in (*sorted(range(2, n_box, 2), key=lambda d: (d.bit_count(), -d)), *range(n_box - 1, 0, -2), 0):
-
-            @pl.when(lax.rem(q + d, 2) == h)
-            def _(h=h, d=d):
-                send_t(h, d).start()
+        for e in (3, 2, 1, 0):
+            pltpu.make_async_remote_copy(
+                src_ref=mine_ref.at[h],
+                dst_ref=t_ref.at[q],
+                send_sem=t_send.at[2 * e + lax.rem(h + side, 2)],
+                recv_sem=t_recv.at[2 * e + lax.rem(h + side, 2)],
+                device_id={"blk": mate, "box": across(2 * e)["box"] - side + h},
+                device_id_type=MESH,
+            ).start()
 
     below = deep_right(jnp.concatenate([l_ref[0], l_ref[1]], axis=1))
     for h in range(2):

time: 21.1 us -> 21 us (level)
  no operation moved by 1% of the time
where the time goes in v9:
time: 21 us; the launch traced here: 20.8 us
  Pallas kernels  20.2 us (96%)
  local copies, waits for them, and re-layouts  0.66 us (3%)
    pallas_call x1, Pallas kernels, on_device(): pl.pallas_call(functools.partial(kernel, n_blk, n_box), out_shape=jax.Sha...  20.2 us
    unnamed x1, local copies, waits for them, and re-layouts  0.66 us

profile of v9, /device:TPU:0, one launch (start us, length us, event | category | flops | bytes accessed | tf_op | source)
XLA Modules:
  0.0 20.8 jit_solution(13643017030277648318)
XLA Ops:
  0.0 20.2 %shard_map.73 = f32[2,16,1024]{2,1,0:T(8,128)S(1)} custom-call(f32[3,128]{1,0:T(4,128)} %points_hbm.1, s32[1,128]{1,0:T(1,128)} %bitcast.1, s32[1,8]{1,0:T(1,128)} %mask_hbm.1, s32[1,32]{1,0:T(1,128)} %skeleton_hbm.1, f32[1,2,128,128]{3,2,1,0:T(8,128)} %l_hbm.1, f32[1,8,2,32,128]{4,3,2,1,0:T(8,128)} %e_hbm.1, f32[1,2,32,256]{3,2,1,0:T(8,128)} %g_hbm.1), custom_call_target="tpu_custom_call" | custom-call | tf_op jit(solution)/shard_map/pallas_call | solution.py:409
  20.2 0.7 %copy.9 = f32[2,16,1024]{2,1,0:T(8,128)} copy(f32[2,16,1024]{2,1,0:T(8,128)S(1)} %shard_map.73) | data formatting | bytes 262144
